TPU v7x, 32 devices: a whole 2x2x4 slice. The times are simulated.
32 devices in a mesh: dp: 16 (over z, y, x), section: 2 (over core).
Axes of the slice: x: 2, y: 2, z: 4, core: 2. Of those that a mesh axis runs over, the one named last changes fastest.
Arguments:
- acts: bfloat16 [2, 32, 256, 512], P('section', 'dp'), may hold values from -6 to 6
- present: int32 [32], P('dp'), may hold values 0 or 1
- embed: bfloat16 [32, 2048], P('dp'), may hold values from -6 to 6
- context: bfloat16 [32, 4, 512], P('dp'), may hold values from -6 to 6
- norm1_gain: float32 [2, 512], P('section'), may hold values from 0.25 to 1.75
- norm1_bias: float32 [2, 512], P('section'), may hold values from -3 to 3
- conv1_weight: bfloat16 [2, 4608, 512], P('section'), may hold values from -0.09375 to 0.09375
- conv1_bias: float32 [2, 512], P('section'), may hold values from -3 to 3
- emb_weight: bfloat16 [2, 2048, 1024], P('section'), may hold values from -0.125 to 0.125
- emb_bias: float32 [2, 1024], P('section'), may hold values from -3 to 3
- norm2_gain: float32 [2, 512], P('section'), may hold values from 0.25 to 1.75
- norm2_bias: float32 [2, 512], P('section'), may hold values from -3 to 3
- conv2_weight: bfloat16 [2, 4608, 512], P('section'), may hold values from -0.09375 to 0.09375
- conv2_bias: float32 [2, 512], P('section'), may hold values from -3 to 3
- norm3_gain: float32 [2, 512], P('section'), may hold values from 0.25 to 1.75
- norm3_bias: float32 [2, 512], P('section'), may hold values from -3 to 3
- qkv_weight: bfloat16 [2, 512, 1536], P('section'), may hold values from -0.25 to 0.25
- context_weight: bfloat16 [2, 512, 1024], P('section'), may hold values from -0.25 to 0.25
- out_weight: bfloat16 [2, 512, 512], P('section'), may hold values from -1 to 1
- out_bias: float32 [2, 512], P('section'), may hold values from -3 to 3
Outputs:
- result: float32 [2, 32, 256, 512], P('section', 'dp')
- grad_norm1_gain: float32 [2, 512], P('section', 'dp')
- grad_norm1_bias: float32 [2, 512], P('section', 'dp')
- grad_conv1_weight: float32 [2, 4608, 512], P('section', 'dp')
- grad_conv1_bias: float32 [2, 512], P('section', 'dp')
- grad_emb_weight: float32 [2, 2048, 1024], P('section', 'dp')
- grad_emb_bias: float32 [2, 1024], P('section', 'dp')
- grad_norm2_gain: float32 [2, 512], P('section', 'dp')
- grad_norm2_bias: float32 [2, 512], P('section', 'dp')
- grad_conv2_weight: float32 [2, 4608, 512], P('section', 'dp')
- grad_conv2_bias: float32 [2, 512], P('section', 'dp')
- grad_norm3_gain: float32 [2, 512], P('section', 'dp')
- grad_norm3_bias: float32 [2, 512], P('section', 'dp')
- grad_qkv_weight: float32 [2, 512, 1536], P('section', 'dp')
- grad_context_weight: float32 [2, 512, 1024], P('section', 'dp')
- grad_out_weight: float32 [2, 512, 512], P('section', 'dp')
- grad_out_bias: float32 [2, 512], P('section', 'dp')
All inputs are finite; a program needn't handle non-finite values. No bound on the sum of `present` on one device may be relied on, other than what follows from the above.
Results may differ from a plain program's by a relative error of at most 0.017.
Values may be sent and summed in bfloat16 or wider, within the bound.
No kernel may reach another device: no remote copies, remote signals or barrier semaphores. Data moves between devices by JAX's collectives and lax.ppermute only.
A program may use at most 448 MiB of HBM per device.

v0:
```python
import jax
import jax.numpy as jnp
from jax import lax
from jax.sharding import PartitionSpec as P

HEADS = 8
HEAD = 64
GROUPS = 32
IMG = 16
MB = 2


EPSILON = 1e-05


def passed_along(value, axis, steps):
    count = lax.axis_size(axis)
    first, last = (max(0, -steps), min(count, count - steps))
    return lax.ppermute(value, axis, [(source, source + steps) for source in range(first, last)])


def silu_of(values):
    return values * jax.nn.sigmoid(values)


def matmul(left, right):
    return jnp.dot(left, right, preferred_element_type=jnp.float32)


def outer_sum(left, right):
    return lax.dot_general(
        left, right, (((0,), (0,)), ((), ())), preferred_element_type=jnp.float32
    )


def times_transposed(left, right):
    return lax.dot_general(
        left, right, (((1,), (1,)), ((), ())), preferred_element_type=jnp.float32
    )


def group_norm(values, scaling, offset):
    number, pixels, channels = values.shape
    grouped = values.reshape(number, pixels, GROUPS, channels // GROUPS)
    average = jnp.mean(grouped, axis=(1, 3), keepdims=True)
    centered = grouped - average
    variance = jnp.mean(centered * centered, axis=(1, 3), keepdims=True)
    return (centered * lax.rsqrt(variance + EPSILON)).reshape(values.shape) * scaling + offset


def front_piece(inputs, scaling, offset):
    return silu_of(group_norm(inputs, scaling, offset))


def middle_piece(hidden, scaling, offset, modulation):
    channels = hidden.shape[2]
    normed = group_norm(hidden, scaling, offset)
    return silu_of(normed * (1.0 + modulation[:, None, :channels]) + modulation[:, None, channels:])


def patches_of(field_in):
    number, pixels, channels = field_in.shape
    grid_view = field_in.reshape(number, IMG, IMG, channels)
    padded = jnp.pad(grid_view, ((0, 0), (1, 1), (1, 1), (0, 0)))
    pieces = [
        padded[:, row_off : row_off + IMG, col_off : col_off + IMG, :]
        for row_off in range(3)
        for col_off in range(3)
    ]
    return jnp.concatenate(pieces, axis=3).reshape(number * pixels, 9 * channels)


def unpatch(grad_patch, number, pixels, channels):
    unused_out, pullback = jax.vjp(patches_of, jnp.zeros((number, pixels, channels), jnp.float32))
    return pullback(grad_patch)[0]


def heads_of(triple, extra_kv):
    number, pixels, triple_width = triple.shape
    channels = triple_width // 3
    queries = triple[:, :, :channels].reshape(number, pixels, HEADS, HEAD)
    key_rows = jnp.concatenate(
        [triple[:, :, channels : 2 * channels], extra_kv[:, :, :channels]], axis=1
    )
    value_rows = jnp.concatenate([triple[:, :, 2 * channels :], extra_kv[:, :, channels:]], axis=1)
    key_rows = key_rows.reshape(number, key_rows.shape[1], HEADS, HEAD)
    value_rows = value_rows.reshape(number, value_rows.shape[1], HEADS, HEAD)
    return (queries, key_rows, value_rows)


def attn_scores(queries, key_rows):
    return jnp.einsum(
        "sqhd,skhd->shqk", queries, key_rows, preferred_element_type=jnp.float32
    ) * HEAD ** (-0.5)


def forward_layer(inputs, embed_m, context_m, weights):
    (
        norm1_gain,
        norm1_bias,
        conv1_weight,
        conv1_bias,
        emb_weight,
        emb_bias,
        norm2_gain,
        norm2_bias,
        conv2_weight,
        conv2_bias,
        norm3_gain,
        norm3_bias,
        qkv_weight,
        context_weight,
        out_weight,
        out_bias,
    ) = weights
    number, pixels, channels = inputs.shape
    first_act = front_piece(inputs, norm1_gain, norm1_bias).astype(jnp.bfloat16)
    hidden = (
        matmul(patches_of(first_act), conv1_weight).reshape(number, pixels, channels) + conv1_bias
    )
    emb_act = silu_of(embed_m.astype(jnp.float32)).astype(jnp.bfloat16)
    modulation = matmul(emb_act, emb_weight) + emb_bias
    second_act = middle_piece(hidden, norm2_gain, norm2_bias, modulation).astype(jnp.bfloat16)
    branch = (
        matmul(patches_of(second_act), conv2_weight).reshape(number, pixels, channels) + conv2_bias
    )
    residual = inputs + branch
    normed = group_norm(residual, norm3_gain, norm3_bias).astype(jnp.bfloat16)
    triple = matmul(normed.reshape(number * pixels, channels), qkv_weight).astype(jnp.bfloat16)
    triple = triple.reshape(number, pixels, 3 * channels)
    extra_kv = jnp.einsum(
        "snc,cd->snd", context_m, context_weight, preferred_element_type=jnp.float32
    ).astype(jnp.bfloat16)
    queries, key_rows, value_rows = heads_of(triple, extra_kv)
    scores = attn_scores(queries, key_rows)
    highest = jnp.max(scores, axis=-1, keepdims=True)
    log_total = highest + jnp.log(jnp.sum(jnp.exp(scores - highest), axis=-1, keepdims=True))
    prob_b = jnp.exp(scores - log_total).astype(jnp.bfloat16)
    attended = jnp.einsum("shqk,skhd->sqhd", prob_b, value_rows, preferred_element_type=jnp.float32)
    attended = attended.astype(jnp.bfloat16).reshape(number * pixels, channels)
    projected = matmul(attended, out_weight).reshape(number, pixels, channels) + out_bias
    saved_list = (
        inputs,
        first_act,
        hidden,
        emb_act,
        modulation,
        second_act,
        residual,
        normed,
        triple,
        extra_kv,
        log_total,
        attended,
    )
    return (residual + projected, saved_list)


def blank_saved(number, pixels, channels, emb_width, extra_count):
    bf16 = jnp.bfloat16
    f32 = jnp.float32
    return (
        jnp.zeros((number, pixels, channels), f32),
        jnp.zeros((number, pixels, channels), bf16),
        jnp.zeros((number, pixels, channels), f32),
        jnp.zeros((number, emb_width), bf16),
        jnp.zeros((number, 2 * channels), f32),
        jnp.zeros((number, pixels, channels), bf16),
        jnp.zeros((number, pixels, channels), f32),
        jnp.zeros((number, pixels, channels), bf16),
        jnp.zeros((number, pixels, 3 * channels), bf16),
        jnp.zeros((number, extra_count, 2 * channels), bf16),
        jnp.zeros((number, HEADS, pixels, 1), f32),
        jnp.zeros((number * pixels, channels), bf16),
    )


def backward_layer(saved_list, grad_out, context_m, weights):
    (
        norm1_gain,
        norm1_bias,
        conv1_weight,
        conv1_bias,
        emb_weight,
        emb_bias,
        norm2_gain,
        norm2_bias,
        conv2_weight,
        conv2_bias,
        norm3_gain,
        norm3_bias,
        qkv_weight,
        context_weight,
        out_weight,
        out_bias,
    ) = weights
    (
        inputs,
        first_act,
        hidden,
        emb_act,
        modulation,
        second_act,
        residual,
        normed,
        triple,
        extra_kv,
        log_total,
        attended,
    ) = saved_list
    number, pixels, channels = inputs.shape
    grad_b = grad_out.astype(jnp.bfloat16).reshape(number * pixels, channels)
    g_out_weight = outer_sum(attended, grad_b)
    g_out_bias = jnp.sum(grad_b.astype(jnp.float32), axis=0)
    d_att = (
        times_transposed(grad_b, out_weight)
        .astype(jnp.bfloat16)
        .reshape(number, pixels, HEADS, HEAD)
    )
    queries, key_rows, value_rows = heads_of(triple, extra_kv)
    prob_f = jnp.exp(attn_scores(queries, key_rows) - log_total)
    prob_b = prob_f.astype(jnp.bfloat16)
    d_probs = jnp.einsum("sqhd,skhd->shqk", d_att, value_rows, preferred_element_type=jnp.float32)
    row_dot = jnp.sum(prob_f * d_probs, axis=-1, keepdims=True)
    d_scores = (prob_f * (d_probs - row_dot)).astype(jnp.bfloat16)
    d_queries = jnp.einsum(
        "shqk,skhd->sqhd", d_scores, key_rows, preferred_element_type=jnp.float32
    ) * HEAD ** (-0.5)
    d_keys = jnp.einsum(
        "shqk,sqhd->skhd", d_scores, queries, preferred_element_type=jnp.float32
    ) * HEAD ** (-0.5)
    d_values = jnp.einsum("shqk,sqhd->skhd", prob_b, d_att, preferred_element_type=jnp.float32)
    extra_count = extra_kv.shape[1]
    d_triple = jnp.concatenate(
        [
            d_queries.reshape(number, pixels, channels),
            d_keys[:, :pixels].reshape(number, pixels, channels),
            d_values[:, :pixels].reshape(number, pixels, channels),
        ],
        axis=2,
    ).astype(jnp.bfloat16)
    d_extra = jnp.concatenate(
        [
            d_keys[:, pixels:].reshape(number, extra_count, channels),
            d_values[:, pixels:].reshape(number, extra_count, channels),
        ],
        axis=2,
    ).astype(jnp.bfloat16)
    d_triple = d_triple.reshape(number * pixels, 3 * channels)
    g_qkv = outer_sum(normed.reshape(number * pixels, channels), d_triple)
    g_context = jnp.einsum("snc,snd->cd", context_m, d_extra, preferred_element_type=jnp.float32)
    d_normed = times_transposed(d_triple, qkv_weight).reshape(number, pixels, channels)
    unused_three, pull_three = jax.vjp(group_norm, residual, norm3_gain, norm3_bias)
    d_resid_add, g_norm3_gain, g_norm3_bias = pull_three(d_normed)
    d_resid = grad_out + d_resid_add
    d_branch = d_resid.astype(jnp.bfloat16).reshape(number * pixels, channels)
    g_conv2 = outer_sum(patches_of(second_act), d_branch)
    g_conv2_bias = jnp.sum(d_branch.astype(jnp.float32), axis=0)
    d_second = unpatch(times_transposed(d_branch, conv2_weight), number, pixels, channels)
    unused_two, pull_two = jax.vjp(middle_piece, hidden, norm2_gain, norm2_bias, modulation)
    d_hidden, g_norm2_gain, g_norm2_bias, d_modul = pull_two(d_second)
    d_modul_b = d_modul.astype(jnp.bfloat16)
    g_emb = outer_sum(emb_act, d_modul_b)
    g_emb_bias = jnp.sum(d_modul_b.astype(jnp.float32), axis=0)
    d_hidden_b = d_hidden.astype(jnp.bfloat16).reshape(number * pixels, channels)
    g_conv1 = outer_sum(patches_of(first_act), d_hidden_b)
    g_conv1_bias = jnp.sum(d_hidden_b.astype(jnp.float32), axis=0)
    d_first = unpatch(times_transposed(d_hidden_b, conv1_weight), number, pixels, channels)
    unused_one, pull_one = jax.vjp(front_piece, inputs, norm1_gain, norm1_bias)
    d_in_add, g_norm1_gain, g_norm1_bias = pull_one(d_first)
    grads = (
        g_norm1_gain,
        g_norm1_bias,
        g_conv1,
        g_conv1_bias,
        g_emb,
        g_emb_bias,
        g_norm2_gain,
        g_norm2_bias,
        g_conv2,
        g_conv2_bias,
        g_norm3_gain,
        g_norm3_bias,
        g_qkv,
        g_context,
        g_out_weight,
        g_out_bias,
    )
    return (d_resid + d_in_add, grads)


def body(
    acts,
    present,
    embed,
    context,
    norm1_gain,
    norm1_bias,
    conv1_weight,
    conv1_bias,
    emb_weight,
    emb_bias,
    norm2_gain,
    norm2_bias,
    conv2_weight,
    conv2_bias,
    norm3_gain,
    norm3_bias,
    qkv_weight,
    context_weight,
    out_weight,
    out_bias,
):
    weights = tuple(
        (
            weight_arg[0]
            for weight_arg in (
                norm1_gain,
                norm1_bias,
                conv1_weight,
                conv1_bias,
                emb_weight,
                emb_bias,
                norm2_gain,
                norm2_bias,
                conv2_weight,
                conv2_bias,
                norm3_gain,
                norm3_bias,
                qkv_weight,
                context_weight,
                out_weight,
                out_bias,
            )
        )
    )
    section_id = lax.axis_index("section")
    is_first = section_id == 0
    images_dev = acts.shape[1]
    pixels = acts.shape[2]
    channels = acts.shape[3]
    per_batch = images_dev // MB
    emb_width = embed.shape[1]
    extra_count = context.shape[1]
    mask_f = present.astype(jnp.float32)[:, None, None]
    source = acts[0].astype(jnp.float32)
    cotan = source * mask_f

    def pick(array, batch_idx):
        return lax.dynamic_slice_in_dim(array, batch_idx * per_batch, per_batch, 0)

    def zero_field():
        return jnp.zeros((per_batch, pixels, channels), jnp.float32)

    received = zero_field()
    outputs = jnp.zeros((images_dev, pixels, channels), jnp.float32)
    stash_list = []
    for step_now in range(MB + 1):
        batch_raw = step_now - section_id
        active = (batch_raw >= 0) & (batch_raw < MB)
        batch_idx = jnp.clip(batch_raw, 0, MB - 1)
        layer_in = jnp.where(is_first, pick(source, batch_idx), received)
        embed_m = pick(embed, batch_idx)
        context_m = pick(context, batch_idx)
        layer_out, saved_list = lax.cond(
            active,
            lambda field_in, embed_in, context_in: forward_layer(
                field_in, embed_in, context_in, weights
            ),
            lambda field_in, embed_in, context_in: (
                zero_field(),
                blank_saved(per_batch, pixels, channels, emb_width, extra_count),
            ),
            layer_in,
            embed_m,
            context_m,
        )
        stash_list.append(saved_list)
        if step_now < MB:
            sending = (layer_out + layer_in).astype(jnp.bfloat16)
            received = passed_along(sending, "section", 1).astype(jnp.float32)
        current = pick(outputs, batch_idx)
        outputs = lax.dynamic_update_slice_in_dim(
            outputs, jnp.where(active, layer_out, current), batch_idx * per_batch, 0
        )

    def zero_grads():
        return tuple((jnp.zeros(weight_arg.shape, jnp.float32) for weight_arg in weights))

    back_recv = zero_field()
    grad_input = jnp.zeros((images_dev, pixels, channels), jnp.float32)
    totals = zero_grads()
    shards = None
    for step_now in range(MB + 1):
        batch_raw = MB - step_now - section_id
        active = (batch_raw >= 0) & (batch_raw < MB)
        batch_idx = jnp.clip(batch_raw, 0, MB - 1)
        grad_out = jnp.where(is_first, back_recv, pick(cotan, batch_idx))
        embed_m = pick(embed, batch_idx)
        context_m = pick(context, batch_idx)
        stashed = stash_list[MB - step_now]
        d_inputs, grads = lax.cond(
            active,
            lambda saved_in, grad_in, embed_in, context_in: backward_layer(
                saved_in, grad_in, context_in, weights
            ),
            lambda saved_in, grad_in, embed_in, context_in: (zero_field(), zero_grads()),
            stashed,
            grad_out,
            embed_m,
            context_m,
        )
        if step_now < MB:
            back_recv = passed_along(d_inputs.astype(jnp.bfloat16), "section", -1).astype(
                jnp.float32
            )
        current = pick(grad_input, batch_idx)
        grad_input = lax.dynamic_update_slice_in_dim(
            grad_input, jnp.where(active, d_inputs + grad_out, current), batch_idx * per_batch, 0
        )
        totals = tuple((acc_a + add_b for acc_a, add_b in zip(totals, grads)))
    shards = lax.psum_scatter(
        tuple((grad_one[None] for grad_one in totals)), "dp", scatter_dimension=1, tiled=True
    )
    result = jnp.where(is_first, grad_input, outputs * mask_f)[None]
    return (result,) + tuple(shards)


def solution(mesh):
    in_specs = (
        P("section", "dp", None, None),
        P("dp"),
        P("dp", None),
        P("dp", None, None),
        P("section", None),
        P("section", None),
        P("section", None, None),
        P("section", None),
        P("section", None, None),
        P("section", None),
        P("section", None),
        P("section", None),
        P("section", None, None),
        P("section", None),
        P("section", None),
        P("section", None),
        P("section", None, None),
        P("section", None, None),
        P("section", None, None),
        P("section", None),
    )
    out_specs = (
        P("section", "dp", None, None),
        P("section", "dp"),
        P("section", "dp"),
        P("section", "dp", None),
        P("section", "dp"),
        P("section", "dp", None),
        P("section", "dp"),
        P("section", "dp"),
        P("section", "dp"),
        P("section", "dp", None),
        P("section", "dp"),
        P("section", "dp"),
        P("section", "dp"),
        P("section", "dp", None),
        P("section", "dp", None),
        P("section", "dp", None),
        P("section", "dp"),
    )
    return jax.shard_map(body, mesh=mesh, in_specs=in_specs, out_specs=out_specs, check_vma=False)
```

profile of v0, /device:TPU:0, one launch (start us, length us, event | category | flops | bytes accessed | tf_op | source)
XLA Modules:
  0.0 2026.9 jit_solution(4372685429300895639)
XLA Ops:
  10.8 25.5 %conditional.6 = (f32[1,256,512]{2,1,0:T(8,128)S(1)}, f32[1,256,512]{2,1,0:T(8,128)S(1)}, bf16[1,256,512]{2,1,0:T(8,128)(2,1)S(1)}, f32[1,256,512]{2,1,0:T(8,128...) conditional(s32[]{:T(128)} %convert_element_type.403, () %tuple.67, ...), branch_computations={%region_0.1_spmd, %region_1.16_spmd} | conditional | flops 3111484928 | bytes 93564480 | solution.py:365
  44.2 30.7 %conditional.7 = (f32[1,256,512]{2,1,0:T(8,128)}, f32[1,256,512]{2,1,0:T(8,128)S(1)}, bf16[1,256,512]{2,1,0:T(8,128)(2,1)S(1)}, f32[1,256,512]{2,1,0:T(8,128)S(1...) conditional(s32[]{:T(128)} %convert_element_type.402, () %tuple.66, ...), branch_computations={%region_16.17_spmd, %region_17.32_spmd} | conditional | flops 3111484928 | bytes 84717184 | solution.py:365
  86.7 25.8 %conditional.9 = (f32[1,256,512]{2,1,0:T(8,128)}, f32[512]{0:T(512)S(1)}, f32[512]{0:T(512)S(1)}, f32[4608,512]{1,0:T(8,128)}, f32[512]{0:T(512)S(1)}, /*index=5...) conditional(s32[]{:T(128)} %convert_element_type.399, () %tuple.64, ...), branch_computations={%region_48.49_spmd, %region_49.86_spmd} | conditional | flops 6280940544 | bytes 235468256 | solution.py:402
  115.4 121.8 %collective-permute-done.2 = bf16[1,256,512]{2,1,0:T(8,128)(2,1)S(1)} collective-permute-done((bf16[1,256,512]{2,1,0:T(8,128)(2,1)S(1)}, bf16[1,256,512]{2,1,0:T(8,128)(2,1)S(1)}, u32[]{:S(2)}, u32[]{:S(2)}) %collective-permute-start.2) | collective-permute-done | bytes 262176 | tf_op jit(solution)/shard_map/ppermute | solution.py:19
  238.1 93.4 %conditional.10 = (f32[1,256,512]{2,1,0:T(8,128)}, f32[512]{0:T(512)}, f32[512]{0:T(512)}, f32[4608,512]{1,0:T(8,128)}, f32[512]{0:T(512)}, /*index=5*/f32[1024]...) conditional(s32[]{:T(128)} %convert_element_type.402, () %tuple.72, ...), branch_computations={%region_86.87_spmd, %region_87.124_spmd} | conditional | flops 6280940544 | bytes 228881984 | solution.py:402
  339.7 98.8 %conditional.11 = (f32[1,256,512]{2,1,0:T(8,128)S(1)}, f32[512]{0:T(512)}, f32[512]{0:T(512)}, f32[4608,512]{1,0:T(8,128)}, f32[512]{0:T(512)}, /*index=5*/f32[1...) conditional(s32[]{:T(128)} %convert_element_type.403, () %tuple.74, ...), branch_computations={%region_124.125_spmd, %region_125.162_spmd} | conditional | flops 6280940544 | bytes 232035808 | solution.py:402
  467.3 13.7 add_bitcast_fusion.2
  481.1 14.9 add_bitcast_fusion.1
  496.0 14.8 add_bitcast_fusion
  521.0 73.5 %reduce-scatter.51.cloned.1.call-done = f32[32,1]{1,0:T(8,128)} async-done(((f32[512,1]{1,0:T(8,128)}), f32[32,1]{1,0:T(8,128)}) %reduce-scatter.51.cloned.1.call-update) | async-done | bytes 144
  595.8 73.4 %reduce-scatter.53.cloned.1.call-done = f32[32,1]{1,0:T(8,128)} async-done(((f32[512,1]{1,0:T(8,128)}), f32[32,1]{1,0:T(8,128)}) %reduce-scatter.53.cloned.1.call-update) | async-done | bytes 144
  670.5 73.4 %reduce-scatter.57.cloned.1.call-done = f32[32,1]{1,0:T(8,128)} async-done(((f32[512,1]{1,0:T(8,128)}), f32[32,1]{1,0:T(8,128)}) %reduce-scatter.57.cloned.1.call-update) | async-done | bytes 144
  745.2 73.3 %reduce-scatter.59.cloned.1.call-done = f32[32,1]{1,0:T(8,128)} async-done(((f32[512,1]{1,0:T(8,128)}), f32[32,1]{1,0:T(8,128)}) %reduce-scatter.59.cloned.1.call-update) | async-done | bytes 144
  819.8 73.4 %reduce-scatter.61.cloned.1.call-done = f32[32,1]{1,0:T(8,128)} async-done(((f32[512,1]{1,0:T(8,128)}), f32[32,1]{1,0:T(8,128)}) %reduce-scatter.61.cloned.1.call-update) | async-done | bytes 144
  894.5 73.4 %reduce-scatter.63.cloned.1.call-done = f32[32,1]{1,0:T(8,128)} async-done(((f32[512,1]{1,0:T(8,128)}), f32[32,1]{1,0:T(8,128)}) %reduce-scatter.63.cloned.1.call-update) | async-done | bytes 144
  969.2 73.5 %reduce-scatter.65.cloned.1.call-done = f32[32,1]{1,0:T(8,128)} async-done(((f32[512,1]{1,0:T(8,128)}), f32[32,1]{1,0:T(8,128)}) %reduce-scatter.65.cloned.1.call-update) | async-done | bytes 144
  1044.0 73.4 %reduce-scatter.67.cloned.1.call-done = f32[32,1]{1,0:T(8,128)} async-done(((f32[512,1]{1,0:T(8,128)}), f32[32,1]{1,0:T(8,128)}) %reduce-scatter.67.cloned.1.call-update) | async-done | bytes 144
  1118.7 73.8 %reduce-scatter.55.cloned.1.call-done = f32[64,1]{1,0:T(8,128)} async-done(((f32[1024,1]{1,0:T(8,128)}), f32[64,1]{1,0:T(8,128)}) %reduce-scatter.55.cloned.1.call-update) | async-done | bytes 272
  1193.9 75.5 %reduce-scatter.47.cloned.1.call-done = f32[1,32,512]{2,1,0:T(8,128)} async-done(((f32[1,512,512]{2,1,0:T(8,128)}), f32[1,32,512]{2,1,0:T(8,128)}) %reduce-scatter.47.cloned.1.call-update) | async-done | bytes 65552 | tf_op jit(solution)/shard_map/reduce_scatter | solution.py:422
  1269.4 80.1 %reduce-scatter.45.cloned.1.call-done = f32[1,32,1024]{2,1,0:T(8,128)} async-done(((f32[1,512,1024]{2,1,0:T(8,128)}), f32[1,32,1024]{2,1,0:T(8,128)}) %reduce-scatter.45.cloned.1.call-update) | async-done | bytes 131088 | tf_op jit(solution)/shard_map/reduce_scatter | solution.py:422
  1349.5 134.0 %reduce-scatter.43.cloned.1.call-done = f32[1,32,1536]{2,1,0:T(8,128)} async-done(((f32[1,512,1536]{2,1,0:T(8,128)}), f32[1,32,1536]{2,1,0:T(8,128)}) %reduce-scatter.43.cloned.1.call-update) | async-done | bytes 196624 | tf_op jit(solution)/shard_map/reduce_scatter | solution.py:422
  1483.5 179.9 %reduce-scatter.39.cloned.1.call-done = f32[1,128,1024]{2,1,0:T(8,128)} async-done(((f32[1,2048,1024]{2,1,0:T(8,128)}), f32[1,128,1024]{2,1,0:T(8,128)}) %reduce-scatter.39.cloned.1.call-update) | async-done | bytes 524304 | tf_op jit(solution)/shard_map/reduce_scatter | solution.py:422
  1663.4 180.7 %reduce-scatter.37.cloned.1.call-done = f32[1,288,512]{2,1,0:T(8,128)} async-done(((f32[1,4608,512]{2,1,0:T(8,128)}), f32[1,288,512]{2,1,0:T(8,128)}) %reduce-scatter.37.cloned.1.call-update) | async-done | bytes 589840 | tf_op jit(solution)/shard_map/reduce_scatter | solution.py:422
  1844.0 175.9 %reduce-scatter.41.cloned.1.call-done = f32[1,288,512]{2,1,0:T(8,128)} async-done(((f32[1,4608,512]{2,1,0:T(8,128)}), f32[1,288,512]{2,1,0:T(8,128)}) %reduce-scatter.41.cloned.1.call-update) | async-done | bytes 589840 | tf_op jit(solution)/shard_map/reduce_scatter | solution.py:422
  (891 shorter events, 356.5 us)
Async XLA Ops:
  7.3 512.4 %reduce-scatter.49.cloned.1.call-start = ((), (), s32[]{:S(2)}) async-start(), calls=%async_computation.22 | async-start | bytes 278528
  39.7 2.8 collective-permute-start
  77.1 2.8 collective-permute-start.1
  112.5 124.9 %copy-start.178 = (f32[512]{0:T(512)}, f32[512]{0:T(512)S(1)}, u32[]{:S(2)}) copy-start(f32[512]{0:T(512)S(1)} %get-tuple-element.745) | copy-start | bytes 6148
  112.5 124.9 %copy-start.170 = (f32[512]{0:T(512)}, f32[512]{0:T(512)S(1)}, u32[]{:S(2)}) copy-start(f32[512]{0:T(512)S(1)} %get-tuple-element.769) | copy-start | bytes 6148
  112.5 124.9 %copy-start.172 = (f32[512]{0:T(512)}, f32[512]{0:T(512)S(1)}, u32[]{:S(2)}) copy-start(f32[512]{0:T(512)S(1)} %get-tuple-element.757) | copy-start | bytes 6148
  112.5 124.9 %copy-start.174 = (f32[512]{0:T(512)}, f32[512]{0:T(512)S(1)}, u32[]{:S(2)}) copy-start(f32[512]{0:T(512)S(1)} %get-tuple-element.754) | copy-start | bytes 6148
  114.1 123.1 %collective-permute-start.2 = (bf16[1,256,512]{2,1,0:T(8,128)(2,1)S(1)}, bf16[1,256,512]{2,1,0:T(8,128)(2,1)S(1)}, u32[]{:S(2)}, u32[]{:S(2)}) collective-permute-start(bf16[1,256,512]{2,1,0:T(8,128)(2,1)S(1)} %get-tuple-element.1320), channel_id=1, source_target_pairs={{1,0},{3,2},{5,4},{7,6},{9,8},{11,10},{13,12},{15,14},{17,16},{19,... | collective-permute-start | bytes 786440 | tf_op jit(solution)/shard_map/ppermute | solution.py:19
  334.4 3.4 collective-permute-start.3
  440.7 153.8 %reduce-scatter.51.cloned.1.call-start = ((), (), s32[]{:S(2)}) async-start(), calls=%async_computation.23 | async-start | bytes 278528
  442.4 226.9 %reduce-scatter.53.cloned.1.call-start = ((), (), s32[]{:S(2)}) async-start(), calls=%async_computation.24 | async-start | bytes 278528
  444.0 299.9 %reduce-scatter.57.cloned.1.call-start = ((), (), s32[]{:S(2)}) async-start(), calls=%async_computation.26 | async-start | bytes 278528
  445.6 372.9 %reduce-scatter.59.cloned.1.call-start = ((), (), s32[]{:S(2)}) async-start(), calls=%async_computation.27 | async-start | bytes 278528
  447.2 445.9 %reduce-scatter.61.cloned.1.call-start = ((), (), s32[]{:S(2)}) async-start(), calls=%async_computation.28 | async-start | bytes 278528
  448.2 519.6 %reduce-scatter.63.cloned.1.call-start = ((), (), s32[]{:S(2)}) async-start(), calls=%async_computation.29 | async-start | bytes 278528
  449.2 593.5 %reduce-scatter.65.cloned.1.call-start = ((), (), s32[]{:S(2)}) async-start(), calls=%async_computation.30 | async-start | bytes 278528
  450.2 667.2 %reduce-scatter.67.cloned.1.call-start = ((), (), s32[]{:S(2)}) async-start(), calls=%async_computation.31 | async-start | bytes 278528
  451.2 741.4 %reduce-scatter.55.cloned.1.call-start = ((), (), s32[]{:S(2)}) async-start(), calls=%async_computation.25 | async-start | bytes 557056
  452.3 817.1 %reduce-scatter.47.cloned.1.call-start = ((), (), s32[]{:S(2)}) async-start(), calls=%async_computation.21 | async-start | bytes 1114112 | tf_op jit(solution)/shard_map/reduce_scatter | solution.py:422
  455.6 893.9 %reduce-scatter.45.cloned.1.call-start = ((), (), s32[]{:S(2)}) async-start(), calls=%async_computation.20 | async-start | bytes 2228224 | tf_op jit(solution)/shard_map/reduce_scatter | solution.py:422
  460.8 1022.7 %reduce-scatter.43.cloned.1.call-start = ((), (), s32[]{:S(2)}) async-start(), calls=%async_computation.19 | async-start | bytes 3342336 | tf_op jit(solution)/shard_map/reduce_scatter | solution.py:422
  467.2 1196.2 %reduce-scatter.39.cloned.1.call-start = ((), (), s32[]{:S(2)}) async-start(), calls=%async_computation.17 | async-start | bytes 8912896 | tf_op jit(solution)/shard_map/reduce_scatter | solution.py:422
  481.0 1363.0 %reduce-scatter.37.cloned.1.call-start = ((), (), s32[]{:S(2)}) async-start(), calls=%async_computation.16 | async-start | bytes 10027008 | tf_op jit(solution)/shard_map/reduce_scatter | solution.py:422
  496.0 1524.0 %reduce-scatter.41.cloned.1.call-start = ((), (), s32[]{:S(2)}) async-start(), calls=%async_computation.18 | async-start | bytes 10027008 | tf_op jit(solution)/shard_map/reduce_scatter | solution.py:422
  (173 other events, 1806.9 us)
Sparse Core Ops, SparseCore 0:
  440.8 78.8 reduce-scatter.48
  522.0 72.4 reduce-scatter.50
  596.8 72.3 reduce-scatter.52
  671.4 72.4 reduce-scatter.56
  746.0 72.4 reduce-scatter.58
  820.7 72.4 reduce-scatter.60
  895.4 72.4 reduce-scatter.62
  970.2 72.4 reduce-scatter.64
  1044.9 72.3 reduce-scatter.66
  1119.6 72.9 reduce-scatter.54
  1195.4 73.9 reduce-scatter.46
  1272.2 77.2 reduce-scatter.44
  1355.8 127.6 reduce-scatter.42
  1486.3 177.0 reduce-scatter.38
  1670.4 173.5 reduce-scatter.36
  1850.2 169.7 reduce-scatter.40
where the time goes:
time: 2040 us; the launch traced here: 2030 us
  waiting for transfers between devices  1620 us (79%)
  local copies, waits for them, and re-layouts  152 us (7%)
  other arithmetic  126 us (6%)
  matrix products  101 us (5%)
    reduce_scatter x6, waiting for transfers between devices, body(): lax.psum_scatter(tuple((grad_one[None] for grad_one in totals)), 'dp', sc...  826 us
    unnamed x26, waiting for transfers between devices  667 us
    ppermute x4, waiting for transfers between devices, passed_along(): lax.ppermute(value, axis, [(source, source + steps) for source in range(f...  125 us
    broadcast_in_dim x6, other arithmetic, body(): grad_one[None]  58.1 us
  transfers between devices with their start and end apart: 20, of which 19 were waited for; matrix products, arithmetic and copies ran while one was open for 4% of the time, Pallas kernels for 0%

commit v1 on v0

--- a/solution.py
+++ b/solution.py
@@ -248,7 +248,6 @@
     ).astype(jnp.bfloat16)
     d_triple = d_triple.reshape(number * pixels, 3 * channels)
     g_qkv = outer_sum(normed.reshape(number * pixels, channels), d_triple)
-    g_context = jnp.einsum("snc,snd->cd", context_m, d_extra, preferred_element_type=jnp.float32)
     d_normed = times_transposed(d_triple, qkv_weight).reshape(number, pixels, channels)
     unused_three, pull_three = jax.vjp(group_norm, residual, norm3_gain, norm3_bias)
     d_resid_add, g_norm3_gain, g_norm3_bias = pull_three(d_normed)
@@ -260,8 +259,6 @@
     unused_two, pull_two = jax.vjp(middle_piece, hidden, norm2_gain, norm2_bias, modulation)
     d_hidden, g_norm2_gain, g_norm2_bias, d_modul = pull_two(d_second)
     d_modul_b = d_modul.astype(jnp.bfloat16)
-    g_emb = outer_sum(emb_act, d_modul_b)
-    g_emb_bias = jnp.sum(d_modul_b.astype(jnp.float32), axis=0)
     d_hidden_b = d_hidden.astype(jnp.bfloat16).reshape(number * pixels, channels)
     g_conv1 = outer_sum(patches_of(first_act), d_hidden_b)
     g_conv1_bias = jnp.sum(d_hidden_b.astype(jnp.float32), axis=0)
@@ -273,8 +270,6 @@
         g_norm1_bias,
         g_conv1,
         g_conv1_bias,
-        g_emb,
-        g_emb_bias,
         g_norm2_gain,
         g_norm2_bias,
         g_conv2,
@@ -282,11 +277,41 @@
         g_norm3_gain,
         g_norm3_bias,
         g_qkv,
-        g_context,
         g_out_weight,
         g_out_bias,
     )
-    return (d_resid + d_in_add, grads)
+    return (d_resid + d_in_add, grads, d_modul_b, d_extra)
+
+
+def halved_sums(arrays, axis):
+    count = lax.axis_size(axis)
+    index = lax.axis_index(axis)
+    bits = [1 << k for k in range(count.bit_length() - 1)]
+    orders = (bits, bits[1::-1] + bits[2:], bits[2:] + bits[:2])
+    state = []
+    for number, array in enumerate(arrays):
+        state.append((array, bits, orders[number % 3]))
+    for step in range(len(bits)):
+        held = []
+        for array, left, order in state:
+            bit = order[step]
+            above = len([one for one in left if one > bit])
+            view = array.reshape((1 << above, 2, array.shape[0] >> (above + 1)) + array.shape[1:])
+            mine = (index // bit) % 2
+            keep = lax.dynamic_index_in_dim(view, mine, 1, keepdims=False)
+            send = lax.dynamic_index_in_dim(view, 1 - mine, 1, keepdims=False).astype(jnp.bfloat16)
+            got = lax.ppermute(send, axis, [(one, one ^ bit) for one in range(count)])
+            held.append((keep, got, [one for one in left if one != bit], order))
+        state = [
+            ((keep + got.astype(jnp.float32)).reshape((-1,) + keep.shape[2:]), left, order)
+            for keep, got, left, order in held
+        ]
+    return [array[0] for array, left, order in state]
+
+
+def two_parts(values):
+    high = values.astype(jnp.bfloat16)
+    return jnp.concatenate([high, (values - high.astype(jnp.float32)).astype(jnp.bfloat16)], axis=1)
 
 
 def body(
@@ -384,13 +409,16 @@
             outputs, jnp.where(active, layer_out, current), batch_idx * per_batch, 0
         )
 
+    kept = [place for place in range(len(weights)) if place not in (4, 5, 13)]
+
     def zero_grads():
-        return tuple((jnp.zeros(weight_arg.shape, jnp.float32) for weight_arg in weights))
+        return tuple((jnp.zeros(weights[place].shape, jnp.float32) for place in kept))
 
     back_recv = zero_field()
     grad_input = jnp.zeros((images_dev, pixels, channels), jnp.float32)
     totals = zero_grads()
-    shards = None
+    d_mod_all = jnp.zeros((images_dev, 2 * channels), jnp.bfloat16)
+    d_extra_all = jnp.zeros((images_dev, extra_count, 2 * channels), jnp.bfloat16)
     for step_now in range(MB + 1):
         batch_raw = MB - step_now - section_id
         active = (batch_raw >= 0) & (batch_raw < MB)
@@ -399,12 +427,17 @@
         embed_m = pick(embed, batch_idx)
         context_m = pick(context, batch_idx)
         stashed = stash_list[MB - step_now]
-        d_inputs, grads = lax.cond(
+        d_inputs, grads, d_mod, d_extra = lax.cond(
             active,
             lambda saved_in, grad_in, embed_in, context_in: backward_layer(
                 saved_in, grad_in, context_in, weights
             ),
-            lambda saved_in, grad_in, embed_in, context_in: (zero_field(), zero_grads()),
+            lambda saved_in, grad_in, embed_in, context_in: (
+                zero_field(),
+                zero_grads(),
+                jnp.zeros((per_batch, 2 * channels), jnp.bfloat16),
+                jnp.zeros((per_batch, extra_count, 2 * channels), jnp.bfloat16),
+            ),
             stashed,
             grad_out,
             embed_m,
@@ -419,9 +452,78 @@
             grad_input, jnp.where(active, d_inputs + grad_out, current), batch_idx * per_batch, 0
         )
         totals = tuple((acc_a + add_b for acc_a, add_b in zip(totals, grads)))
-    shards = lax.psum_scatter(
-        tuple((grad_one[None] for grad_one in totals)), "dp", scatter_dimension=1, tiled=True
-    )
+        d_mod_all = lax.dynamic_update_slice_in_dim(
+            d_mod_all,
+            jnp.where(active, d_mod, pick(d_mod_all, batch_idx)),
+            batch_idx * per_batch,
+            0,
+        )
+        d_extra_all = lax.dynamic_update_slice_in_dim(
+            d_extra_all,
+            jnp.where(active, d_extra, pick(d_extra_all, batch_idx)),
+            batch_idx * per_batch,
+            0,
+        )
+    count = lax.axis_size("dp")
+
+    def by_shard(array):
+        return array.reshape((count, array.shape[0] // count) + array.shape[1:])
+
+    total_of = dict(zip(kept, totals))
+    rest = jnp.concatenate(
+        [by_shard(total_of[12]), by_shard(total_of[14])], axis=2
+    )
+    conv1_shard, conv2_shard, rest_shard = halved_sums(
+        [by_shard(total_of[2]), by_shard(total_of[8]), rest], "dp"
+    )
+    vector_at = [place for place in kept if weights[place].ndim == 1]
+    vectors = jnp.concatenate([by_shard(total_of[place]) for place in vector_at], axis=1)
+    width = vectors.shape[1]
+    wide = 2 * channels
+    emb_act = silu_of(embed.astype(jnp.float32)).astype(jnp.bfloat16)
+    emb_cols = emb_width // count
+    context_cols = channels // count
+
+    def split_columns(array, columns):
+        return array.reshape(-1, count, columns).swapaxes(0, 1).reshape(count, -1)
+
+    early = jnp.concatenate(
+        [
+            split_columns(emb_act, emb_cols),
+            split_columns(context.reshape(-1, channels), context_cols),
+        ],
+        axis=1,
+    )
+    early = lax.all_to_all(early, "dp", 0, 0)
+    emb_part = early[:, : images_dev * emb_cols].reshape(count * images_dev, emb_cols)
+    context_part = early[:, images_dev * emb_cols :].reshape(-1, context_cols)
+    same = jnp.concatenate([d_mod_all.reshape(-1), d_extra_all.reshape(-1)])
+    late = jnp.concatenate(
+        [two_parts(vectors), jnp.broadcast_to(same[None], (count, same.shape[0]))], axis=1
+    )
+    late = lax.all_to_all(late, "dp", 0, 0)
+    summed = jnp.sum(late[:, : 2 * width].astype(jnp.float32), axis=0)
+    summed = summed[:width] + summed[width:]
+    d_mod_g = late[:, 2 * width : 2 * width + images_dev * wide].reshape(-1, wide)
+    d_extra_g = late[:, 2 * width + images_dev * wide :].reshape(-1, wide)
+    each = channels // count
+    vector_of = {
+        place: summed[number * each : (number + 1) * each]
+        for number, place in enumerate(vector_at)
+    }
+    emb_bias_all = jnp.sum(d_mod_g.astype(jnp.float32), axis=0)
+    emb_bias_shard = lax.dynamic_slice_in_dim(
+        emb_bias_all, lax.axis_index("dp") * (wide // count), wide // count, 0
+    )
+    shard_of = dict(vector_of)
+    shard_of[2] = conv1_shard
+    shard_of[8] = conv2_shard
+    shard_of[4] = outer_sum(emb_part, d_mod_g)
+    shard_of[5] = emb_bias_shard
+    shard_of[12] = rest_shard[:, : 3 * channels]
+    shard_of[13] = outer_sum(context_part, d_extra_g)
+    shard_of[14] = rest_shard[:, 3 * channels :]
+    shards = [shard_of[place][None] for place in range(len(weights))]
     result = jnp.where(is_first, grad_input, outputs * mask_f)[None]
     return (result,) + tuple(shards)
 

time: 2040 us -> 535 us (0.26)
  waiting for transfers between devices: 1620 us -> 154 us
  local copies, waits for them, and re-layouts: 152 us -> 117 us
  starting transfers between devices: 6.45 us -> 35.9 us
    reduce_scatter x6 -> x0, waiting for transfers between devices: 826 us -> none  [body(): lax.psum_scatter(tuple((grad_one[None] for grad_one in totals)), 'dp', sc...]
    unnamed x26 -> x0, waiting for transfers between devices: 667 us -> none
    broadcast_in_dim x6 -> x0, other arithmetic: 58.1 us -> none  [body(): grad_one[None]]
    ppermute x0 -> x12, waiting for transfers between devices: none -> 51.9 us  [halved_sums(): got = lax.ppermute(send, axis, [(one, one ^ bit) for one in range(count)])]
    add x10 -> x13, other arithmetic: 3.49 us -> 34 us  [body(): totals = tuple((acc_a + add_b for acc_a, add_b in zip(totals, grads)))]
    ppermute x4, waiting for transfers between devices: 125 us -> 94.9 us  [passed_along(): lax.ppermute(value, axis, [(source, source + steps) for source in range(f...]
    cond x6 -> x2, local copies, waits for them, and re-layouts: 32.2 us -> 7.59 us  [body(): lax.cond(active, lambda saved_in, grad_in, embed_in, context_in: backward...]
  transfers between devices with their start and end apart: 20 -> 18, of which waited for: 19 -> 9; matrix products, arithmetic and copies ran while one was open for 4% -> 11% of each run, Pallas kernels for 0% -> 0%
where the time goes in v1:
time: 535 us; the launch traced here: 526 us
  waiting for transfers between devices  154 us (29%)
  local copies, waits for them, and re-layouts  117 us (22%)
  other arithmetic  111 us (21%)
  matrix products  97.3 us (18%)
  starting transfers between devices  35.9 us (7%)
  loops' own time  8.38 us (2%)
    ppermute x4, waiting for transfers between devices, passed_along(): lax.ppermute(value, axis, [(source, source + steps) for source in range(f...  94.9 us
    ppermute x12, waiting for transfers between devices, halved_sums(): got = lax.ppermute(send, axis, [(one, one ^ bit) for one in range(count)])  51.9 us
    dot_general x10, matrix products, outer_sum(): lax.dot_general(left, right, (((0,), (0,)), ((), ())), preferred_element_...  36.9 us
    add x13, other arithmetic, body(): totals = tuple((acc_a + add_b for acc_a, add_b in zip(totals, grads)))  34 us
    cond x267, local copies, waits for them, and re-layouts  28.9 us
    dot_general x10, matrix products, matmul(): return jnp.dot(left, right, preferred_element_type=jnp.float32)  24.9 us
    another operation x34, local copies, waits for them, and re-layouts  20.5 us
    dot_general x8, matrix products, times_transposed(): lax.dot_general(left, right, (((1,), (1,)), ((), ())), preferred_element_...  20.3 us
  transfers between devices with their start and end apart: 18, of which 9 were waited for; matrix products, arithmetic and copies ran while one was open for 11% of the time, Pallas kernels for 0%

profile of v1, /device:TPU:0, one launch (start us, length us, event | category | flops | bytes accessed | tf_op | source)
XLA Modules:
  0.0 526.1 jit_solution(2383956776752556834)
XLA Ops:
  4.8 25.6 %conditional.6 = (f32[1,256,512]{2,1,0:T(8,128)S(1)}, f32[1,256,512]{2,1,0:T(8,128)S(1)}, bf16[1,256,512]{2,1,0:T(8,128)(2,1)S(1)}, f32[1,256,512]{2,1,0:T(8,128...) conditional(s32[]{:T(128)} %convert_element_type.601, () %tuple.71, ...), branch_computations={%region_0.1_spmd, %region_1.16_spmd} | conditional | flops 3111484928 | bytes 92479000 | solution.py:390
  40.0 31.2 %conditional.7 = (f32[1,256,512]{2,1,0:T(8,128)}, f32[1,256,512]{2,1,0:T(8,128)S(1)}, bf16[1,256,512]{2,1,0:T(8,128)(2,1)S(1)}, f32[1,256,512]{2,1,0:T(8,128)S(1...) conditional(s32[]{:T(128)} %convert_element_type.600, () %tuple.70, ...), branch_computations={%region_16.17_spmd, %region_17.32_spmd} | conditional | flops 3111484928 | bytes 85778136 | solution.py:390
  50.8 4.5 fusion.220
  77.1 8.3 %all-to-all-start.1 = ((bf16[16,2,256]{2,1,0:T(2,128)(2,1)}), bf16[16,2,256]{2,1,0:T(2,128)(2,1)S(1)}, u32[]{:S(2)}, u32[]{:S(2)}) async-start(bf16[16,2,256]{2,1,0:T(2,128)(2,1)} %reshape.4874), calls=%async_computation.1 | async-start | bytes 32768 | tf_op jit(solution)/shard_map/all_to_all | solution.py:497
  85.6 7.2 %all-to-all-done.1 = bf16[16,2,256]{2,1,0:T(2,128)(2,1)S(1)} async-done(((bf16[16,2,256]{2,1,0:T(2,128)(2,1)}), bf16[16,2,256]{2,1,0:T(2,128)(2,1)S(1)}, u32[]{:S(2)}, u32[]{:S(2)}) %all-to-all-start.1) | async-done | bytes 16416 | tf_op jit(solution)/shard_map/all_to_all | solution.py:497
  94.3 5.7 %conditional.8 = (f32[1,256,512]{2,1,0:T(8,128)S(1)}, f32[1,256,512]{2,1,0:T(8,128)S(1)}, bf16[1,256,512]{2,1,0:T(8,128)(2,1)}, f32[1,256,512]{2,1,0:T(8,128)S(1...) conditional(s32[]{:T(128)} %convert_element_type.597, () %tuple.69, ...), branch_computations={%region_32.33_spmd, %region_33.48_spmd} | conditional | flops 3111616000 | bytes 90586664 | solution.py:390
  100.8 18.5 %conditional.9 = (f32[1,256,512]{2,1,0:T(8,128)S(1)}, f32[512]{0:T(512)S(1)}, f32[512]{0:T(512)S(1)}, f32[4608,512]{1,0:T(8,128)}, f32[512]{0:T(512)S(1)}, /*ind...) conditional(s32[]{:T(128)} %convert_element_type.597, () %tuple.68, ...), branch_computations={%region_48.49_spmd, %region_49.86_spmd} | conditional | flops 6274646016 | bytes 204919904 | solution.py:430
  104.1 4.7 broadcast.3021.clone
  108.8 4.8 broadcast.3021
  124.0 93.2 %collective-permute-done.2 = bf16[1,256,512]{2,1,0:T(8,128)(2,1)S(1)} collective-permute-done((bf16[1,256,512]{2,1,0:T(8,128)(2,1)S(1)}, bf16[1,256,512]{2,1,0:T(8,128)(2,1)S(1)}, u32[]{:S(2)}, u32[]{:S(2)}) %collective-permute-start.2) | collective-permute-done | bytes 262176 | tf_op jit(solution)/shard_map/ppermute | solution.py:19
  218.4 76.1 %conditional.10 = (f32[1,256,512]{2,1,0:T(8,128)}, f32[512]{0:T(512)}, f32[512]{0:T(512)}, f32[4608,512]{1,0:T(8,128)}, f32[512]{0:T(512)}, /*index=5*/f32[512]{...) conditional(s32[]{:T(128)} %convert_element_type.600, () %tuple.76, ...), branch_computations={%region_86.87_spmd, %region_87.124_spmd} | conditional | flops 6274646016 | bytes 202602912 | solution.py:430
  282.5 6.9 %fusion.121 = f32[4608,512]{1,0:T(8,128)} fusion(bf16[256,4608]{1,0:T(8,128)(2,1)} %constant_dynamic-update-slice_fusion.67, bf16[1,256,512]{2,1,0:T(8,128)(2,1)S(1)} %get-tuple-element.1283), kind=kOutput, calls=%fused_computation.484 | convolution fusion | flops 1207959552 | bytes 12058624 | tf_op jit(solution)/shard_map/cond/branch_1_fun/dot_general | solution.py:31
  289.4 5.1 fusion.119
  302.7 78.7 %conditional.11 = (f32[1,256,512]{2,1,0:T(8,128)S(1)}, f32[512]{0:T(512)}, f32[512]{0:T(512)S(1)}, f32[4608,512]{1,0:T(8,128)}, f32[512]{0:T(512)S(1)}, /*index=...) conditional(s32[]{:T(128)} %convert_element_type.601, () %tuple.78, ...), branch_computations={%region_124.125_spmd, %region_125.162_spmd} | conditional | flops 6274646016 | bytes 203725376 | solution.py:430
  369.1 7.0 %fusion.156 = f32[4608,512]{1,0:T(8,128)} fusion(bf16[256,4608]{1,0:T(8,128)(2,1)} %constant_dynamic-update-slice_fusion.83, bf16[1,256,512]{2,1,0:T(8,128)(2,1)S(1)} %get-tuple-element.1291), kind=kOutput, calls=%fused_computation.623 | convolution fusion | flops 1207959552 | bytes 12058624 | tf_op jit(solution)/shard_map/cond/branch_1_fun/dot_general | solution.py:31
  376.1 5.1 fusion.154
  403.2 10.9 %add_add_fusion.15 = f32[4608,512]{1,0:T(8,128)S(1)} fusion(f32[4608,512]{1,0:T(8,128)} %get-tuple-element.834, f32[4608,512]{1,0:T(8,128)} %get-tuple-element.832, f32[4608,512]{1,0:T(8,128)} %get-tuple-element.833), kind=kLoop, calls=%fused_computation.670 | loop fusion | flops 4718592 | bytes 37748736 | tf_op jit(solution)/shard_map/add | solution.py:454
  418.5 11.1 %add_add_fusion.16 = f32[4608,512]{1,0:T(8,128)S(1)} fusion(f32[4608,512]{1,0:T(8,128)} %get-tuple-element.831, f32[4608,512]{1,0:T(8,128)} %get-tuple-element.829, f32[4608,512]{1,0:T(8,128)} %get-tuple-element.830), kind=kLoop, calls=%fused_computation.671 | loop fusion | flops 4718592 | bytes 37748736 | tf_op jit(solution)/shard_map/add | solution.py:454
  441.6 9.8 %collective-permute-done.13 = bf16[1,4,32,2048]{3,2,1,0:T(8,128)(2,1)} collective-permute-done((bf16[1,4,32,2048]{3,2,1,0:T(8,128)(2,1)S(1)}, bf16[1,4,32,2048]{3,2,1,0:T(8,128)(2,1)}, u32[]{:S(2)}, u32[]{:S(2)}) %collective-permute-start.13) | collective-permute-done | bytes 524320 | tf_op jit(solution)/shard_map/ppermute | solution.py:303
  455.5 8.1 %collective-permute-done.14 = bf16[2,1,32,2048]{3,2,0,1:T(8,128)(2,1)S(1)} collective-permute-done((bf16[2,1,32,2048]{3,2,0,1:T(8,128)(2,1)S(1)}, bf16[2,1,32,2048]{3,2,0,1:T(8,128)(2,1)S(1)}, u32[]{:S(2)}, u32[]{:S(2)}) %collective-permute-start.14) | collective-permute-done | bytes 262176 | tf_op jit(solution)/shard_map/ppermute | solution.py:303
  479.0 13.8 %collective-permute-done.15 = bf16[1,1,32,2048]{3,2,0,1:T(8,128)(2,1)S(1)} collective-permute-done((bf16[1,1,32,2048]{3,2,0,1:T(8,128)(2,1)S(1)}, bf16[1,1,32,2048]{3,2,0,1:T(8,128)(2,1)S(1)}, u32[]{:S(2)}, u32[]{:S(2)}) %collective-permute-start.15) | collective-permute-done | bytes 131104 | tf_op jit(solution)/shard_map/ppermute | solution.py:303
  500.1 5.3 %collective-permute-done.10 = bf16[2,1,288,512]{3,2,0,1:T(8,128)(2,1)S(1)} collective-permute-done((bf16[2,1,288,512]{3,2,0,1:T(8,128)(2,1)S(1)}, bf16[2,1,288,512]{3,2,0,1:T(8,128)(2,1)S(1)}, u32[]{:S(2)}, u32[]{:S(2)}) %collective-permute-start.10) | collective-permute-done | bytes 589856 | tf_op jit(solution)/shard_map/ppermute | solution.py:303
  508.2 6.8 %collective-permute-done.6 = bf16[2,1,288,512]{3,2,0,1:T(8,128)(2,1)S(1)} collective-permute-done((bf16[2,1,288,512]{3,2,0,1:T(8,128)(2,1)S(1)}, bf16[2,1,288,512]{3,2,0,1:T(8,128)(2,1)S(1)}, u32[]{:S(2)}, u32[]{:S(2)}) %collective-permute-start.6) | collective-permute-done | bytes 589856 | tf_op jit(solution)/shard_map/ppermute | solution.py:303
  516.8 8.2 %collective-permute-done.7 = bf16[1,1,288,512]{3,2,0,1:T(8,128)(2,1)S(1)} collective-permute-done((bf16[1,1,288,512]{3,2,0,1:T(8,128)(2,1)S(1)}, bf16[1,1,288,512]{3,2,0,1:T(8,128)(2,1)S(1)}, u32[]{:S(2)}, u32[]{:S(2)}) %collective-permute-start.7) | collective-permute-done | bytes 294944 | tf_op jit(solution)/shard_map/ppermute | solution.py:303
  (914 shorter events, 294.6 us)
Async XLA Ops:
  35.3 3.0 collective-permute-start
  73.7 20.5 %collective-permute-start.1 = (bf16[1,256,512]{2,1,0:T(8,128)(2,1)}, bf16[1,256,512]{2,1,0:T(8,128)(2,1)S(1)}, u32[]{:S(2)}, u32[]{:S(2)}) collective-permute-start(bf16[1,256,512]{2,1,0:T(8,128)(2,1)} %get-tuple-element.1542), channel_id=1, source_target_pairs={{0,1},{2,3},{4,5},{6,7},{8,9},{10,11},{12,13},{14,15},{16,17},{18,... | collective-permute-start | bytes 786440 | tf_op jit(solution)/shard_map/ppermute | solution.py:19
  77.1 15.7 %all-to-all-start.1 = ((bf16[16,2,256]{2,1,0:T(2,128)(2,1)}), bf16[16,2,256]{2,1,0:T(2,128)(2,1)S(1)}, u32[]{:S(2)}, u32[]{:S(2)}) async-start(bf16[16,2,256]{2,1,0:T(2,128)(2,1)} %reshape.4874), calls=%async_computation.1 | async-start | bytes 32768 | tf_op jit(solution)/shard_map/all_to_all | solution.py:497
  119.3 99.0 %copy-start.182 = (f32[512]{0:T(512)}, f32[512]{0:T(512)S(1)}, u32[]{:S(2)}) copy-start(f32[512]{0:T(512)S(1)} %get-tuple-element.805) | copy-start | bytes 6148
  119.4 99.0 %copy-start.183 = (f32[512]{0:T(512)}, f32[512]{0:T(512)S(1)}, u32[]{:S(2)}) copy-start(f32[512]{0:T(512)S(1)} %get-tuple-element.802) | copy-start | bytes 6148
  119.4 99.0 %copy-start.184 = (f32[512]{0:T(512)}, f32[512]{0:T(512)S(1)}, u32[]{:S(2)}) copy-start(f32[512]{0:T(512)S(1)} %get-tuple-element.799) | copy-start | bytes 6148
  119.4 99.0 %copy-start.185 = (f32[512]{0:T(512)}, f32[512]{0:T(512)S(1)}, u32[]{:S(2)}) copy-start(f32[512]{0:T(512)S(1)} %get-tuple-element.796) | copy-start | bytes 6148
  119.5 98.8 %copy-start.23 = (bf16[1,512,512]{2,1,0:T(8,128)(2,1)S(1)}, bf16[1,512,512]{2,1,0:T(8,128)(2,1)}, u32[]{:S(2)}) copy-start(bf16[1,512,512]{2,1,0:T(8,128)(2,1)} %param.50) | copy-start | bytes 1572868
  119.5 98.8 %copy-start.74 = (bf16[1,256,512]{2,1,0:T(8,128)(2,1)S(1)}, bf16[1,256,512]{2,1,0:T(8,128)(2,1)}, u32[]{:S(2)}) copy-start(bf16[1,256,512]{2,1,0:T(8,128)(2,1)} %copy-done.73) | copy-start | bytes 786436
  120.6 96.6 %collective-permute-start.2 = (bf16[1,256,512]{2,1,0:T(8,128)(2,1)S(1)}, bf16[1,256,512]{2,1,0:T(8,128)(2,1)S(1)}, u32[]{:S(2)}, u32[]{:S(2)}) collective-permute-start(bf16[1,256,512]{2,1,0:T(8,128)(2,1)S(1)} %get-tuple-element.1547), channel_id=1, source_target_pairs={{1,0},{3,2},{5,4},{7,6},{9,8},{11,10},{13,12},{15,14},{17,16},{19,... | collective-permute-start | bytes 786440 | tf_op jit(solution)/shard_map/ppermute | solution.py:19
  297.0 3.8 collective-permute-start.3
  391.5 48.1 %all-to-all-start = ((bf16[16,2,5408]{2,1,0:T(2,128)(2,1)}), bf16[16,2,5408]{2,1,0:T(2,128)(2,1)S(1)}, u32[]{:S(2)}, u32[]{:S(2)}) async-start(bf16[16,2,5408]{2,1,0:T(2,128)(2,1)} %reshape.4872), calls=%async_computation | async-start | bytes 704512 | tf_op jit(solution)/shard_map/all_to_all | solution.py:504
  401.3 31.8 %collective-permute-start.12 = (bf16[2,4,32,2048]{3,2,1,0:T(8,128)(2,1)S(1)}, bf16[2,4,32,2048]{3,2,1,0:T(8,128)(2,1)S(1)}, u32[]{:S(2)}, u32[]{:S(2)}) collective-permute-start(bf16[2,4,32,2048]{3,2,1,0:T(8,128)(2,1)S(1)} %fusion.179), channel_id=1, source_target_pairs={{0,8},{2,10},{4,12},{6,14},{8,0},{10,2},{12,4},{14,6},{16,24},{18,... | collective-permute-start | bytes 3145736 | tf_op jit(solution)/shard_map/ppermute | solution.py:303
  416.0 47.5 %collective-permute-start.8 = (bf16[4,2,288,512]{3,2,1,0:T(8,128)(2,1)}, bf16[4,2,288,512]{3,2,1,0:T(8,128)(2,1)}, u32[]{:S(2)}, u32[]{:S(2)}) collective-permute-start(bf16[4,2,288,512]{3,2,1,0:T(8,128)(2,1)} %fusion.172), channel_id=1, source_target_pairs={{0,4},{2,6},{4,0},{6,2},{8,12},{10,14},{12,8},{14,10},{16,20},{18,... | collective-permute-start | bytes 7077896 | tf_op jit(solution)/shard_map/ppermute | solution.py:303
  431.4 39.0 %collective-permute-start.4 = (bf16[8,1,288,512]{3,2,0,1:T(8,128)(2,1)}, bf16[8,1,288,512]{3,2,0,1:T(8,128)(2,1)}, u32[]{:S(2)}, u32[]{:S(2)}) collective-permute-start(bf16[8,1,288,512]{3,2,0,1:T(8,128)(2,1)} %fusion.171), channel_id=1, source_target_pairs={{0,2},{2,0},{4,6},{6,4},{8,10},{10,8},{12,14},{14,12},{16,18},{18,... | collective-permute-start | bytes 7077896 | tf_op jit(solution)/shard_map/ppermute | solution.py:303
  436.0 15.4 %collective-permute-start.13 = (bf16[1,4,32,2048]{3,2,1,0:T(8,128)(2,1)S(1)}, bf16[1,4,32,2048]{3,2,1,0:T(8,128)(2,1)}, u32[]{:S(2)}, u32[]{:S(2)}) collective-permute-start(bf16[1,4,32,2048]{3,2,1,0:T(8,128)(2,1)S(1)} %dynamic-slice_convert_fusion.6), channel_id=1, source_target_pairs={{0,16},{2,18},{4,20},{6,22},{8,24},{10,26},{12,28},{14,30},{16,0},... | collective-permute-start | bytes 1572872 | tf_op jit(solution)/shard_map/ppermute | solution.py:303
  452.9 10.6 %collective-permute-start.14 = (bf16[2,1,32,2048]{3,2,0,1:T(8,128)(2,1)S(1)}, bf16[2,1,32,2048]{3,2,0,1:T(8,128)(2,1)S(1)}, u32[]{:S(2)}, u32[]{:S(2)}) collective-permute-start(bf16[2,1,32,2048]{3,2,0,1:T(8,128)(2,1)S(1)} %fusion.182), channel_id=1, source_target_pairs={{0,2},{2,0},{4,6},{6,4},{8,10},{10,8},{12,14},{14,12},{16,18},{18,... | collective-permute-start | bytes 786440 | tf_op jit(solution)/shard_map/ppermute | solution.py:303
  468.9 23.9 %collective-permute-start.9 = (bf16[4,1,288,512]{3,2,1,0:T(8,128)(2,1)}, bf16[4,1,288,512]{3,2,1,0:T(8,128)(2,1)}, u32[]{:S(2)}, u32[]{:S(2)}) collective-permute-start(bf16[4,1,288,512]{3,2,1,0:T(8,128)(2,1)} %dynamic-slice_convert_fusion.2), channel_id=1, source_target_pairs={{0,2},{2,0},{4,6},{6,4},{8,10},{10,8},{12,14},{14,12},{16,18},{18,... | collective-permute-start | bytes 3538952 | tf_op jit(solution)/shard_map/ppermute | solution.py:303
  475.1 21.0 %collective-permute-start.5 = (bf16[4,1,288,512]{3,2,0,1:T(8,128)(2,1)S(1)}, bf16[4,1,288,512]{3,2,0,1:T(8,128)(2,1)}, u32[]{:S(2)}, u32[]{:S(2)}) collective-permute-start(bf16[4,1,288,512]{3,2,0,1:T(8,128)(2,1)S(1)} %fusion.178), channel_id=1, source_target_pairs={{0,4},{2,6},{4,0},{6,2},{8,12},{10,14},{12,8},{14,10},{16,20},{18,... | collective-permute-start | bytes 3538952 | tf_op jit(solution)/shard_map/ppermute | solution.py:303
  476.7 16.1 %collective-permute-start.15 = (bf16[1,1,32,2048]{3,2,0,1:T(8,128)(2,1)S(1)}, bf16[1,1,32,2048]{3,2,0,1:T(8,128)(2,1)S(1)}, u32[]{:S(2)}, u32[]{:S(2)}) collective-permute-start(bf16[1,1,32,2048]{3,2,0,1:T(8,128)(2,1)S(1)} %dynamic-slice_convert_fusion.10), channel_id=1, source_target_pairs={{0,4},{2,6},{4,0},{6,2},{8,12},{10,14},{12,8},{14,10},{16,20},{18,... | collective-permute-start | bytes 393224 | tf_op jit(solution)/shard_map/ppermute | solution.py:303
  495.5 9.9 %collective-permute-start.10 = (bf16[2,1,288,512]{3,2,0,1:T(8,128)(2,1)S(1)}, bf16[2,1,288,512]{3,2,0,1:T(8,128)(2,1)S(1)}, u32[]{:S(2)}, u32[]{:S(2)}) collective-permute-start(bf16[2,1,288,512]{3,2,0,1:T(8,128)(2,1)S(1)} %fusion.181), channel_id=1, source_target_pairs={{0,8},{2,10},{4,12},{6,14},{8,0},{10,2},{12,4},{14,6},{16,24},{18,... | collective-permute-start | bytes 1769480 | tf_op jit(solution)/shard_map/ppermute | solution.py:303
  498.0 16.9 %collective-permute-start.6 = (bf16[2,1,288,512]{3,2,0,1:T(8,128)(2,1)S(1)}, bf16[2,1,288,512]{3,2,0,1:T(8,128)(2,1)S(1)}, u32[]{:S(2)}, u32[]{:S(2)}) collective-permute-start(bf16[2,1,288,512]{3,2,0,1:T(8,128)(2,1)S(1)} %fusion.180), channel_id=1, source_target_pairs={{0,8},{2,10},{4,12},{6,14},{8,0},{10,2},{12,4},{14,6},{16,24},{18,... | collective-permute-start | bytes 1769480 | tf_op jit(solution)/shard_map/ppermute | solution.py:303
  505.7 10.2 %collective-permute-start.11 = (bf16[1,1,288,512]{3,2,0,1:T(8,128)(2,1)S(1)}, bf16[1,1,288,512]{3,2,0,1:T(8,128)(2,1)S(1)}, u32[]{:S(2)}, u32[]{:S(2)}) collective-permute-start(bf16[1,1,288,512]{3,2,0,1:T(8,128)(2,1)S(1)} %dynamic-slice_convert_fusion.7), channel_id=1, source_target_pairs={{0,16},{2,18},{4,20},{6,22},{8,24},{10,26},{12,28},{14,30},{16,0},... | collective-permute-start | bytes 884744 | tf_op jit(solution)/shard_map/ppermute | solution.py:303
  515.2 9.8 %collective-permute-start.7 = (bf16[1,1,288,512]{3,2,0,1:T(8,128)(2,1)S(1)}, bf16[1,1,288,512]{3,2,0,1:T(8,128)(2,1)S(1)}, u32[]{:S(2)}, u32[]{:S(2)}) collective-permute-start(bf16[1,1,288,512]{3,2,0,1:T(8,128)(2,1)S(1)} %dynamic-slice_convert_fusion.8), channel_id=1, source_target_pairs={{0,16},{2,18},{4,20},{6,22},{8,24},{10,26},{12,28},{14,30},{16,0},... | collective-permute-start | bytes 884744 | tf_op jit(solution)/shard_map/ppermute | solution.py:303
  (168 other events, 813.2 us)
